TPU v7x, 32 devices: a whole 2x2x4 slice. The times are simulated.
32 devices in a mesh: cell: 4 (over y, x), gene: 8 (over z, core).
Axes of the slice: x: 2, y: 2, z: 4, core: 2. Of those that a mesh axis runs over, the one named last changes fastest.
Arguments:
- counts: float32 [1024, 16384], P('cell', 'gene'), as said below
- gene_mean: float32 [16384], P('gene'), may hold values from -5 to 10
- gene_std: float32 [16384], P('gene'), may hold values from 0 to 10
Outputs:
- gram: float32 [16384, 16384], P('gene', 'cell')
Inputs may be any that keep to these rules, and one draw needn't show every extreme that they name: `counts`: whole numbers; every cell has at least one count.
All inputs are finite; a program needn't handle non-finite values.
Results may differ from a plain program's by a relative error of at most 0.013.
Values may be sent and summed in bfloat16 or wider, within the bound.
No kernel may reach another device: no remote copies, remote signals or barrier semaphores. Data moves between devices by JAX's collectives and lax.ppermute only.
A program may use at most 192 MiB of HBM per device.

v0:
```python
import functools

import jax
import jax.numpy as jnp
from jax import lax
from jax.experimental import pallas as pl
from jax.experimental.pallas import tpu as pltpu
from jax.sharding import PartitionSpec as P

STRIP = 128
SHARES = (3, 3, 2)
TILE = 1024
MIB = 2**20
SLACK = 8
VMEM = pl.BlockSpec(memory_space=pltpu.VMEM)
ANY = pl.BlockSpec(memory_space=pl.ANY)


def send(x, axis, pairs):
    return lax.ppermute(x, axis, pairs)


def call(kernel, name, cost, vmem=8, **kwargs):
    flops, moved, transcendentals = cost
    return pl.pallas_call(
        kernel,
        name=name,
        cost_estimate=pl.CostEstimate(
            flops=flops // SLACK,
            bytes_accessed=moved // SLACK,
            transcendentals=transcendentals // SLACK,
        ),
        compiler_params=pltpu.CompilerParams(vmem_limit_bytes=vmem * MIB),
        **kwargs,
    )


def count_kernel(counts_ref, out_ref, held_ref):
    cells, genes = counts_ref.shape
    total = jnp.zeros((cells, STRIP), jnp.float32)
    for at in range(0, genes, STRIP):
        strip = counts_ref[:, at : at + STRIP]
        held_ref[:, at : at + STRIP] = strip
        total += strip
    summed = jnp.sum(total, axis=1, keepdims=True)
    flat = jnp.broadcast_to(summed, (cells, STRIP)).T
    out_ref[...] = flat[:8, :]


def count_part(counts):
    cells, genes = counts.shape
    return call(
        count_kernel,
        "count_part",
        (cells * genes, 8 * cells * genes, 0),
        vmem=4,
        in_specs=[VMEM],
        out_specs=[VMEM] * 2,
        out_shape=[
            jax.ShapeDtypeStruct((8, cells), jnp.float32),
            jax.ShapeDtypeStruct(counts.shape, jnp.float32),
        ],
    )(counts)


def scales_kernel(mean_ref, std_ref, *refs):
    out_ref = refs[-1]
    out_ref[0:1, :] = mean_ref[...]
    out_ref[8:9, :] = 1.0 / jnp.maximum(std_ref[...], 0.1)


def gene_scales(mean, std, after):
    genes = mean.shape[1]
    return call(
        scales_kernel,
        "gene_scales",
        (2 * genes, 72 * genes, 0),
        vmem=1,
        in_specs=[VMEM] * 2 + [ANY] * len(after),
        out_specs=VMEM,
        out_shape=jax.ShapeDtypeStruct((16, genes), jnp.float32),
    )(mean, std, *after)


def add_kernel(a_ref, b_ref, out_ref):
    out_ref[...] = a_ref[...] + b_ref[...]


def add(a, b):
    return call(
        add_kernel,
        "add_terms",
        (a.size, 12 * a.size, 0),
        vmem=1,
        in_specs=[VMEM] * 2,
        out_specs=VMEM,
        out_shape=jax.ShapeDtypeStruct(a.shape, a.dtype),
    )(a, b)


def library_terms(part, size):
    terms, step = [part], 1
    while step < size:
        part = terms[0] if len(terms) == 1 else add(*terms)
        terms = [part, send(part, "gene", [(g, g ^ step) for g in range(size)])]
        step *= 2
    return terms


def scaled_strip(counts_ref, genes_ref, factor, at):
    normal = jnp.log1p(counts_ref[:, at] * factor)
    return jnp.minimum((normal - genes_ref[0:1, at]) * genes_ref[8:9, at], 10.0)


def cell_factor(sums, cells):
    library = sums[0][:1, :]
    for ref in sums[1:]:
        library = library + ref[:1, :]
    return jnp.broadcast_to(10000.0 / library, (STRIP, cells)).T


def block_kernel(terms, start, counts_ref, genes_ref, *refs):
    factor = cell_factor(refs[:terms], counts_ref.shape[0])
    out_ref = refs[-1]

    @pl.loop(0, out_ref.shape[1] // STRIP)
    def _(k):
        there = pl.multiple_of(k * STRIP, STRIP)
        at = pl.ds(start + there, STRIP)
        scaled = scaled_strip(counts_ref, genes_ref, factor, at)
        out_ref[:, pl.ds(there, STRIP)] = scaled.astype(jnp.bfloat16)


def rows_kernel(terms, counts_ref, genes_ref, *refs):
    factor = cell_factor(refs[:terms], counts_ref.shape[0])
    out_ref = refs[-1]

    @pl.loop(0, counts_ref.shape[1] // STRIP)
    def _(k):
        at = pl.ds(pl.multiple_of(k * STRIP, STRIP), STRIP)
        scaled = scaled_strip(counts_ref, genes_ref, factor, at)
        out_ref[at, :] = scaled.T.astype(jnp.bfloat16)


def standardize(kernel, name, shape, pieces, counts, scales, terms, after=()):
    size = pieces * shape[0] * shape[1]
    return call(
        functools.partial(kernel, len(terms)),
        name,
        (20 * size, 6 * size, size),
        in_specs=[VMEM] * (2 + len(terms)) + [ANY] * len(after),
        out_specs=[VMEM] * pieces,
        out_shape=[jax.ShapeDtypeStruct(shape, jnp.bfloat16)] * pieces,
    )(counts, scales, *terms, *after)


def split_kernel(one_ref, two_ref, *refs):
    top_ref, low_ref = refs[-2:]
    half = top_ref.shape[0]
    top_ref[...] = one_ref[:half, :]
    low_ref[...] = two_ref[half:, :]


def row_blocks(mine, groups, after):
    def cross(x, j):
        return send(x, "cell", [(c, c ^ j) for c in range(groups)])

    if groups != 4:
        return [[mine]] + [[cross(mine, j)] for j in range(1, groups)]
    one, two = cross(mine, 1), cross(mine, 2)
    half = jax.ShapeDtypeStruct((mine.shape[0] // 2, mine.shape[1]), mine.dtype)
    top, low = call(
        split_kernel,
        "split_rows",
        (0, 4 * mine.size, 0),
        vmem=4,
        in_specs=[VMEM] * 2 + [ANY] * len(after),
        out_specs=[VMEM] * 2,
        out_shape=[half] * 2,
    )(one, two, *after)
    return [[mine], [one], [two], [cross(top, 2), cross(low, 1)]]


def stack_kernel(places, *refs):
    out_ref = refs[-1]
    for ref, (line, at) in zip(refs, places):
        high, wide = ref.shape
        out_ref[line : line + high, at : at + wide] = ref[...]


def stack(columns, after=()):
    places, blocks, at = [], [], 0
    for column in columns:
        line = 0
        for x in column:
            places.append((line, at))
            blocks.append(x)
            line += x.shape[0]
        at += column[0].shape[1]
    return call(
        functools.partial(stack_kernel, places),
        "stack_blocks",
        (0, 4 * line * at, 0),
        vmem=4,
        in_specs=[VMEM] * len(blocks) + [ANY] * len(after),
        out_specs=VMEM,
        out_shape=jax.ShapeDtypeStruct((line, at), blocks[0].dtype),
    )(*blocks, *after)


def line_pairs(outer, inner, moves):
    return [(a * inner + i, b * inner + i) for a, b in moves for i in range(inner)]


def line_move(x, outer, inner, moves):
    return send(x, "gene", line_pairs(outer, inner, moves))


def line_near(block, outer, inner):
    if outer == 4:
        return line_move(block, outer, inner, [(0, 1), (1, 0), (2, 3), (3, 2)])
    return line_move(block, outer, inner, [(o, o + 1) for o in range(outer - 1)])


def line_gather(block, near, outer, inner, after):
    def move(x, moves):
        return line_move(x, outer, inner, moves)

    if outer == 4:
        both = stack([[block, near]], after)
        across = move(both, [(1, 2), (2, 1)])
        ends = move(across, [(1, 0), (2, 3)])
        return both, [block, near, across, ends]
    ups, downs = [block, near], [block]
    for h in range(1, outer):
        if h > 1:
            ups.append(move(ups[-1], [(o, o + 1) for o in range(h - 1, outer - 1)]))
        downs.append(move(downs[-1], [(o, o - 1) for o in range(1, outer - h + 1)]))
    return block, [block] + ups[1:] + downs[1:]


def line_place(outer, at, wanted):
    if outer == 4:
        far = {0: (2, 3), 1: (2, 3), 2: (1, 0), 3: (1, 0)}[at]
        if wanted in far:
            return far.index(wanted) + (2 if at in (1, 2) else 4)
        return int(wanted != at)
    if wanted <= at:
        return at - wanted
    return outer - 1 + wanted - at


def pick_kernel(groups, outer, inner, arrays, *refs):
    outs = refs[-groups:]
    depth = outs[0].shape[0]
    sources = [
        (ref, part * depth)
        for ref in refs[:arrays]
        for part in range(ref.shape[0] // depth)
    ]
    cell_at = lax.axis_index("cell")
    line_at = lax.div(lax.axis_index("gene"), jnp.int32(inner))
    pairs = [(o, to) for o in range(outer) for to in range(outer)]
    for j in range(groups):
        here = line_at * outer + lax.bitwise_xor(cell_at, jnp.int32(j))
        for k, (ref, line) in enumerate(sources):
            found = [o * outer + to for o, to in pairs if line_place(outer, o, to) == k]
            match = functools.reduce(jnp.logical_or, [here == x for x in found])

            @pl.when(match)
            def _():
                outs[j][...] = ref[line : line + depth, :]


def pick(arrays, outer, inner, after):
    depth, width = arrays[0].shape
    return call(
        functools.partial(pick_kernel, outer, outer, inner, len(arrays)),
        "pick_blocks",
        (0, 4 * outer * depth * width, 0),
        vmem=4,
        in_specs=[VMEM] * len(arrays) + [ANY] * len(after),
        out_specs=[VMEM] * outer,
        out_shape=[jax.ShapeDtypeStruct((depth, width), arrays[0].dtype)] * outer,
    )(*arrays, *after)


def gram_kernel(inner, steps, start, scale, rows_ref, *refs):
    cols = refs[: len(steps)]
    out_ref, done_ref, tiles, sems = refs[-4:]
    tile, width = tiles.shape[1:]
    genes = rows_ref.shape[0]

    def give(n):
        m, k = divmod(n, len(steps))
        owner = lax.rem(lax.axis_index("gene") + steps[k], jnp.int32(inner))
        at = pl.multiple_of(owner * genes + start, STRIP)
        return pltpu.make_async_copy(
            tiles.at[n % 2],
            out_ref.at[pl.ds(m * tile, tile), pl.ds(at, width)],
            sems.at[n % 2],
        )

    count = genes // tile * len(steps)
    for n in range(count):
        m, k = divmod(n, len(steps))
        if n >= 2:
            give(n - 2).wait()
        total = jnp.dot(
            rows_ref[m * tile : (m + 1) * tile, :],
            cols[k][...],
            preferred_element_type=jnp.float32,
        )
        tiles[n % 2] = total * scale
        give(n).start()
    for n in range(max(count - 2, 0), count):
        give(n).wait()
    done_ref[...] = jnp.zeros_like(done_ref)


def gram_part(gram, steps, start, cols, rows, shape, scale, after=()):
    genes, depth = rows.shape
    width = cols[0].shape[1]
    tile = min(TILE, genes)
    inner = shape[1] // genes
    operands = [rows, *cols, *after]
    in_specs = [VMEM] * (1 + len(cols)) + [ANY] * len(after)
    aliases = {}
    if gram is not None:
        aliases = {len(operands): 0}
        in_specs.append(ANY)
        operands.append(gram)
    return call(
        functools.partial(gram_kernel, inner, steps, start, scale),
        "gram_part",
        (
            2 * len(cols) * genes * depth * width,
            4 * len(cols) * genes * width + 2 * genes * depth,
            0,
        ),
        vmem=24,
        in_specs=in_specs,
        out_specs=[ANY, VMEM],
        out_shape=[
            jax.ShapeDtypeStruct(shape, jnp.float32),
            jax.ShapeDtypeStruct((8, 128), jnp.float32),
        ],
        scratch_shapes=[
            pltpu.VMEM((2, tile, width), jnp.float32),
            pltpu.SemaphoreType.DMA((2,)),
        ],
        input_output_aliases=aliases,
    )(*operands)


def chunks(genes):
    units, spans, at = genes // STRIP, [], 0
    for share in SHARES[:-1]:
        size = max(1, units * share // sum(SHARES))
        spans.append((at * STRIP, size * STRIP))
        at += size
    return spans + [(at * STRIP, (units - at) * STRIP)]


def shards(counts, gene_mean, gene_std):
    groups = lax.axis_size("cell")
    outer, inner = groups, lax.axis_size("gene") // groups
    cells, genes = counts.shape
    part, counts = count_part(counts)
    terms = library_terms(part, outer * inner)
    scales = gene_scales(gene_mean[None, :], gene_std[None, :], [terms[0]])
    given = counts, scales, terms

    spans, blocks, nears, mine = chunks(genes), [], [], []
    for start, width in spans:
        (block,) = standardize(
            lambda terms, *refs, start=start: block_kernel(terms, start, *refs),
            "standardize_block",
            (cells, width),
            1,
            *given,
            [*mine, *blocks[1:]],
        )
        blocks.append(block)
        nears.append(line_near(block, outer, inner))
        if not mine:
            mine = standardize(
                rows_kernel, "standardize_rows", (genes, cells), 1, *given, [block]
            )
    lines, boths = [], []
    for q, (block, near) in enumerate(zip(blocks, nears)):
        after = boths[-1:] + (nears[q + 1 :] if q else [])
        both, arrays = line_gather(block, near, outer, inner, after)
        lines.append(arrays)
        boths.append(both)
    rows = stack(row_blocks(mine[0], groups, boths[1:2]))

    shape = (genes, genes * inner)
    scale = 1.0 / (cells * groups)
    across = [[(c, c ^ j) for c in range(groups)] for j in range(groups)]
    swap = [
        [
            (o * inner + (i + s) % inner, o * inner + i)
            for o in range(outer)
            for i in range(inner)
        ]
        for s in range(inner)
    ]
    write = functools.partial(gram_part, rows=rows, shape=shape, scale=scale)
    gram, done, sent, arrived = None, rows, [], []

    def fetch(q):
        ahead = lines[q + 1][2:3] if q + 1 < len(spans) else []
        sends = pick(lines[q], outer, inner, [done] + sent[-1:] + boths[-1:] + ahead)
        sent.append(sends[0])
        cols = [send(sends[j], "cell", across[j]) for j in range(1, groups)]
        arrived.append([sends[0]] + cols)

    fetch(0)
    for q, (start, _) in enumerate(spans):
        if q + 1 < len(spans):
            fetch(q + 1)
        own = stack([arrived[q]], [done] * (q > 0) + sent[q + 1 : q + 2])
        theirs = [send(own, "gene", swap[s]) for s in range(1, inner)]
        parts = list(enumerate([own] + theirs))
        for part in [parts] if q + 1 < len(spans) else [[x] for x in parts]:
            steps, cols = zip(*part)
            gram, done = write(gram, steps, start, cols, after=sent[q + 1 : q + 2])
    return gram


def solution(mesh):
    placed = (P("cell", "gene"), P("gene"), P("gene"))
    return jax.shard_map(
        shards, mesh=mesh, in_specs=placed, out_specs=P("gene", "cell"), check_vma=False
    )
```

profile of v0, /device:TPU:9, one launch (start us, length us, event | category | flops | bytes accessed | tf_op | source)
XLA Modules:
  0.0 127.2 jit_solution(13357206493636883614)
XLA Ops:
  0.0 1.6 %copy-done = f32[256,2048]{1,0:T(8,128)S(1)} copy-done((f32[256,2048]{1,0:T(8,128)S(1)}, f32[256,2048]{1,0:T(8,128)}, u32[]{:S(2)}) %copy-start) | copy-done | bytes 2097176
  3.4 2.5 %collective-permute-done.1.b_ref = f32[8,256]{1,0:T(8,128)S(1)} collective-permute-done((f32[8,256]{1,0:T(8,128)S(1)}, f32[8,256]{1,0:T(8,128)S(1)}, u32[]{:S(2)}, u32[]{:S(2)}) %collective-permute-start.1) | collective-permute-done | bytes 8224 | tf_op jit(solution)/shard_map/ppermute | solution.py:20
  5.9 2.3 %collective-permute-start.2 = (f32[8,256]{1,0:T(8,128)S(1)}, f32[8,256]{1,0:T(8,128)S(1)}, u32[]{:S(2)}, u32[]{:S(2)}) collective-permute-start(f32[8,256]{1,0:T(8,128)S(1)} %add_terms.3.refs_0_.refs_2_), channel_id=1, source_target_pairs={{0,4},{1,5},{2,6},{3,7},{4,0},{5,1},{6,2},{7,3},{8,12},{9,13},{10,... | collective-permute-start | bytes 24584 | tf_op jit(solution)/shard_map/ppermute | solution.py:20
  8.2 1.1 collective-permute-done.2.refs_3_.refs_1_
  10.0 2.3 %standardize_rows.1.refs_4_.refs_0_ = bf16[2048,256]{1,0:T(8,128)(2,1)S(1)} custom-call(f32[256,2048]{1,0:T(8,128)S(1)} %get-tuple-element.27.refs_0_.counts_ref, f32[16,2048]{1,0:T(8,128)S(1)} %gene_scales.1.refs_1_.genes_ref, f32[8,256]{1,0:T(8,128)S(1)} %add_terms.3.refs_0_.refs_2_, f32[8,256]{1,0:T(8,128)S(1)} %collective-permute-done.2.refs_3_.refs_1_, ...), custom_call_target="tpu_custom_call" | custom-call | flops 1310720 | bytes 393216 | tf_op jit(solution)/shard_map/standardize_rows/pallas_call | solution.py:147
  12.3 1.4 %collective-permute-start.4 = (bf16[2048,256]{1,0:T(8,128)(2,1)S(1)}, bf16[2048,256]{1,0:T(8,128)(2,1)S(1)}, u32[]{:S(2)}, u32[]{:S(2)}) collective-permute-start(bf16[2048,256]{1,0:T(8,128)(2,1)S(1)} %standardize_rows.1.refs_4_.refs_0_), channel_id=1, source_target_pairs={{0,16},{8,24},{16,0},{24,8},{1,17},{9,25},{17,1},{25,9},{2,18},{10... | collective-permute-start | bytes 3145736 | tf_op jit(solution)/shard_map/ppermute | solution.py:20
  13.6 1.2 collective-permute-start.3
  15.4 1.4 %collective-permute-start.5 = (bf16[256,768]{1,0:T(8,128)(2,1)S(1)}, bf16[256,768]{1,0:T(8,128)(2,1)S(1)}, u32[]{:S(2)}, u32[]{:S(2)}) collective-permute-start(bf16[256,768]{1,0:T(8,128)(2,1)S(1)} %standardize_block.4.refs_5_.refs_0_), channel_id=1, source_target_pairs={{0,2},{1,3},{2,0},{3,1},{4,6},{5,7},{6,4},{7,5},{8,10},{9,11},{10,... | collective-permute-start | bytes 1179656 | tf_op jit(solution)/shard_map/ppermute | solution.py:20
  16.7 1.1 collective-permute-done.6.refs_1_
  17.9 3.2 %collective-permute-start.12 = (bf16[512,768]{1,0:T(8,128)(2,1)S(1)}, bf16[512,768]{1,0:T(8,128)(2,1)S(1)}, u32[]{:S(2)}, u32[]{:S(2)}) collective-permute-start(bf16[512,768]{1,0:T(8,128)(2,1)S(1)} %stack_blocks.7.refs_2_), channel_id=1, source_target_pairs={{2,4},{3,5},{4,2},{5,3},{10,12},{11,13},{12,10},{13,11},{18,20},{1... | collective-permute-start | bytes 2359304 | tf_op jit(solution)/shard_map/ppermute | solution.py:20
  21.6 10.7 %collective-permute-done.7.refs_3_.refs_1_ = bf16[256,512]{1,0:T(8,128)(2,1)S(1)} collective-permute-done((bf16[256,512]{1,0:T(8,128)(2,1)S(1)}, bf16[256,512]{1,0:T(8,128)(2,1)S(1)}, u32[]{:S(2)}, u32[]{:S(2)}) %collective-permute-start.7) | collective-permute-done | bytes 262176 | tf_op jit(solution)/shard_map/ppermute | solution.py:20
  32.3 3.7 %collective-permute-start.14 = (bf16[512,768]{1,0:T(8,128)(2,1)S(1)}, bf16[512,768]{1,0:T(8,128)(2,1)S(1)}, u32[]{:S(2)}, u32[]{:S(2)}) collective-permute-start(bf16[512,768]{1,0:T(8,128)(2,1)S(1)} %stack_blocks.8.refs_0_.refs_2_), channel_id=1, source_target_pairs={{2,4},{3,5},{4,2},{5,3},{10,12},{11,13},{12,10},{13,11},{18,20},{1... | collective-permute-start | bytes 2359304 | tf_op jit(solution)/shard_map/ppermute | solution.py:20
  36.1 1.3 %collective-permute-start.13 = (bf16[512,768]{1,0:T(8,128)(2,1)S(1)}, bf16[512,768]{1,0:T(8,128)(2,1)S(1)}, u32[]{:S(2)}, u32[]{:S(2)}) collective-permute-start(bf16[512,768]{1,0:T(8,128)(2,1)S(1)} %collective-permute-done.12.refs_2_), channel_id=1, source_target_pairs={{2,0},{3,1},{4,6},{5,7},{10,8},{11,9},{12,14},{13,15},{18,16},{19,... | collective-permute-start | bytes 2359304 | tf_op jit(solution)/shard_map/ppermute | solution.py:20
  39.1 15.1 %collective-permute-done.14.refs_6_.refs_2_ = bf16[512,768]{1,0:T(8,128)(2,1)S(1)} collective-permute-done((bf16[512,768]{1,0:T(8,128)(2,1)S(1)}, bf16[512,768]{1,0:T(8,128)(2,1)S(1)}, u32[]{:S(2)}, u32[]{:S(2)}) %collective-permute-start.14) | collective-permute-done | bytes 786464 | tf_op jit(solution)/shard_map/ppermute | solution.py:20
  54.2 1.3 %collective-permute-start.18 = (bf16[512,768]{1,0:T(8,128)(2,1)S(1)}, bf16[512,768]{1,0:T(8,128)(2,1)S(1)}, u32[]{:S(2)}, u32[]{:S(2)}) collective-permute-start(bf16[512,768]{1,0:T(8,128)(2,1)S(1)} %collective-permute-done.14.refs_6_.refs_2_), channel_id=1, source_target_pairs={{2,0},{3,1},{4,6},{5,7},{10,8},{11,9},{12,14},{13,15},{18,16},{19,... | collective-permute-start | bytes 2359304 | tf_op jit(solution)/shard_map/ppermute | solution.py:20
  55.6 3.4 %collective-permute-start.10 = (bf16[512,512]{1,0:T(8,128)(2,1)S(1)}, bf16[512,512]{1,0:T(8,128)(2,1)S(1)}, u32[]{:S(2)}, u32[]{:S(2)}) collective-permute-start(bf16[512,512]{1,0:T(8,128)(2,1)S(1)} %stack_blocks.10.refs_5_.refs_6_), channel_id=1, source_target_pairs={{2,4},{3,5},{4,2},{5,3},{10,12},{11,13},{12,10},{13,11},{18,20},{1... | collective-permute-start | bytes 1572872 | tf_op jit(solution)/shard_map/ppermute | solution.py:20
  59.8 0.9 collective-permute-start.15
  61.4 1.1 collective-permute-start.17
  62.5 6.0 %collective-permute-done.10.refs_7_.refs_2_ = bf16[512,512]{1,0:T(8,128)(2,1)S(1)} collective-permute-done((bf16[512,512]{1,0:T(8,128)(2,1)S(1)}, bf16[512,512]{1,0:T(8,128)(2,1)S(1)}, u32[]{:S(2)}, u32[]{:S(2)}) %collective-permute-start.10) | collective-permute-done | bytes 524320 | tf_op jit(solution)/shard_map/ppermute | solution.py:20
  68.5 1.7 %collective-permute-done.18.refs_3_ = bf16[512,768]{1,0:T(8,128)(2,1)S(1)} collective-permute-done((bf16[512,768]{1,0:T(8,128)(2,1)S(1)}, bf16[512,768]{1,0:T(8,128)(2,1)S(1)}, u32[]{:S(2)}, u32[]{:S(2)}) %collective-permute-start.18) | collective-permute-done | bytes 786464 | tf_op jit(solution)/shard_map/ppermute | solution.py:20
  70.4 6.1 %collective-permute-done.17.refs_3_ = bf16[256,768]{1,0:T(8,128)(2,1)S(1)} collective-permute-done((bf16[256,768]{1,0:T(8,128)(2,1)S(1)}, bf16[256,768]{1,0:T(8,128)(2,1)S(1)}, u32[]{:S(2)}, u32[]{:S(2)}) %collective-permute-start.17) | collective-permute-done | bytes 393248 | tf_op jit(solution)/shard_map/ppermute | solution.py:20
  76.7 4.2 %collective-permute-start.19 = (bf16[1024,768]{1,0:T(8,128)(2,1)S(1)}, bf16[1024,768]{1,0:T(8,128)(2,1)S(1)}, u32[]{:S(2)}, u32[]{:S(2)}) collective-permute-start(bf16[1024,768]{1,0:T(8,128)(2,1)S(1)} %stack_blocks.11.refs_0_), channel_id=1, source_target_pairs={{1,0},{0,1},{3,2},{2,3},{5,4},{4,5},{7,6},{6,7},{9,8},{8,9},{11,10... | collective-permute-start | bytes 4718600 | tf_op jit(solution)/shard_map/ppermute | solution.py:20
  80.9 1.3 %collective-permute-start.11 = (bf16[512,512]{1,0:T(8,128)(2,1)S(1)}, bf16[512,512]{1,0:T(8,128)(2,1)S(1)}, u32[]{:S(2)}, u32[]{:S(2)}) collective-permute-start(bf16[512,512]{1,0:T(8,128)(2,1)S(1)} %collective-permute-done.10.refs_7_.refs_2_), channel_id=1, source_target_pairs={{2,0},{3,1},{4,6},{5,7},{10,8},{11,9},{12,14},{13,15},{18,16},{19,... | collective-permute-start | bytes 1572872 | tf_op jit(solution)/shard_map/ppermute | solution.py:20
  83.7 1.2 collective-permute-start.25
  84.9 10.4 %gram_part.4 = (f32[2048,4096]{1,0:T(8,128)}, f32[8,128]{1,0:T(8,128)S(1)}) custom-call(bf16[2048,1024]{1,0:T(8,128)(2,1)S(1)} %stack_blocks.9.refs_4_.rows_ref, bf16[1024,768]{1,0:T(8,128)(2,1)S(1)} %stack_blocks.11.refs_0_, bf16[1024,768]{1,0:T(8,128)(2,1)S(1)} %collective-permute-done.19.refs_1_, ...), custom_call_target="tpu_custom_call" | custom-call | flops 805306368 | bytes 2097152 | tf_op jit(solution)/shard_map/gram_part/pallas_call | solution.py:333
  95.7 6.2 %collective-permute-done.25.refs_3_ = bf16[256,768]{1,0:T(8,128)(2,1)S(1)} collective-permute-done((bf16[256,768]{1,0:T(8,128)(2,1)S(1)}, bf16[256,768]{1,0:T(8,128)(2,1)S(1)}, u32[]{:S(2)}, u32[]{:S(2)}) %collective-permute-start.25) | collective-permute-done | bytes 393248 | tf_op jit(solution)/shard_map/ppermute | solution.py:20
  102.0 1.0 collective-permute-start.26
  104.6 1.1 collective-permute-start.22
  106.1 10.3 %gram_part.5 = (f32[2048,4096]{1,0:T(8,128)}, f32[8,128]{1,0:T(8,128)S(1)}) custom-call(bf16[2048,1024]{1,0:T(8,128)(2,1)S(1)} %stack_blocks.9.refs_4_.rows_ref, bf16[1024,768]{1,0:T(8,128)(2,1)S(1)} %stack_blocks.12.refs_0_, bf16[1024,768]{1,0:T(8,128)(2,1)S(1)} %collective-permute-done.26.refs_1_, ...), custom_call_target="tpu_custom_call", output_to_operand_aliasing={{0}: (4, {})} | custom-call | flops 805306368 | bytes 2097152 | tf_op jit(solution)/shard_map/gram_part/pallas_call | solution.py:333
  117.2 1.2 collective-permute-start.27
  118.4 4.4 %gram_part.6 = (f32[2048,4096]{1,0:T(8,128)}, f32[8,128]{1,0:T(8,128)}) custom-call(bf16[2048,1024]{1,0:T(8,128)(2,1)S(1)} %stack_blocks.9.refs_4_.rows_ref, bf16[1024,512]{1,0:T(8,128)(2,1)S(1)} %stack_blocks.13.refs_0_, f32[2048,4096]{1,0:T(8,128)} %get-tuple-element.46.refs_1_), custom_call_target="tpu_custom_call", output_to_operand_aliasing={{0}: (2, {})} | custom-call | flops 268435456 | bytes 1048576 | tf_op jit(solution)/shard_map/gram_part/pallas_call | solution.py:333
  122.8 4.2 %gram_part.7 = (f32[2048,4096]{1,0:T(8,128)}, f32[8,128]{1,0:T(8,128)}) custom-call(bf16[2048,1024]{1,0:T(8,128)(2,1)S(1)} %stack_blocks.9.refs_4_.rows_ref, bf16[1024,512]{1,0:T(8,128)(2,1)S(1)} %collective-permute-done.27.refs_0_, f32[2048,4096]{1,0:T(8,128)} %get-tuple-element.47.refs_1_), custom_call_target="tpu_custom_call", output_to_operand_aliasing={{0}: (2, {})} | custom-call | flops 268435456 | bytes 1048576 | tf_op jit(solution)/shard_map/gram_part/pallas_call | solution.py:333
  (53 shorter events, 11.9 us)
Async XLA Ops:
  0.0 1.6 %copy-start = (f32[256,2048]{1,0:T(8,128)S(1)}, f32[256,2048]{1,0:T(8,128)}, u32[]{:S(2)}) copy-start(f32[256,2048]{1,0:T(8,128)} %counts_ref.1) | copy-start | bytes 6291460
  1.6 6.6 %copy-start.1 = (f32[2048]{0:T(1024)S(1)}, f32[2048]{0:T(1024)}, u32[]{:S(2)}) copy-start(f32[2048]{0:T(1024)} %param.4) | copy-start | bytes 24580
  1.6 6.6 %copy-start.2 = (f32[2048]{0:T(1024)S(1)}, f32[2048]{0:T(1024)}, u32[]{:S(2)}) copy-start(f32[2048]{0:T(1024)} %param.5) | copy-start | bytes 24580
  1.8 1.5 %collective-permute-start = (f32[8,256]{1,0:T(8,128)S(1)}, f32[8,256]{1,0:T(8,128)S(1)}, u32[]{:S(2)}, u32[]{:S(2)}) collective-permute-start(f32[8,256]{1,0:T(8,128)S(1)} %get-tuple-element.28.a_ref), channel_id=1, source_target_pairs={{0,1},{1,0},{2,3},{3,2},{4,5},{5,4},{6,7},{7,6},{8,9},{9,8},{10,11... | collective-permute-start | bytes 24584 | tf_op jit(solution)/shard_map/ppermute | solution.py:20
  3.4 2.5 %collective-permute-start.1 = (f32[8,256]{1,0:T(8,128)S(1)}, f32[8,256]{1,0:T(8,128)S(1)}, u32[]{:S(2)}, u32[]{:S(2)}) collective-permute-start(f32[8,256]{1,0:T(8,128)S(1)} %add_terms.2.a_ref), channel_id=1, source_target_pairs={{0,2},{1,3},{2,0},{3,1},{4,6},{5,7},{6,4},{7,5},{8,10},{9,11},{10,... | collective-permute-start | bytes 24584 | tf_op jit(solution)/shard_map/ppermute | solution.py:20
  5.9 3.4 %collective-permute-start.2 = (f32[8,256]{1,0:T(8,128)S(1)}, f32[8,256]{1,0:T(8,128)S(1)}, u32[]{:S(2)}, u32[]{:S(2)}) collective-permute-start(f32[8,256]{1,0:T(8,128)S(1)} %add_terms.3.refs_0_.refs_2_), channel_id=1, source_target_pairs={{0,4},{1,5},{2,6},{3,7},{4,0},{5,1},{6,2},{7,3},{8,12},{9,13},{10,... | collective-permute-start | bytes 24584 | tf_op jit(solution)/shard_map/ppermute | solution.py:20
  9.8 8.0 %collective-permute-start.6 = (bf16[256,768]{1,0:T(8,128)(2,1)S(1)}, bf16[256,768]{1,0:T(8,128)(2,1)S(1)}, u32[]{:S(2)}, u32[]{:S(2)}) collective-permute-start(bf16[256,768]{1,0:T(8,128)(2,1)S(1)} %standardize_block.3.refs_2_.refs_0_), channel_id=1, source_target_pairs={{0,2},{1,3},{2,0},{3,1},{4,6},{5,7},{6,4},{7,5},{8,10},{9,11},{10,... | collective-permute-start | bytes 1179656 | tf_op jit(solution)/shard_map/ppermute | solution.py:20
  12.3 25.1 %collective-permute-start.4 = (bf16[2048,256]{1,0:T(8,128)(2,1)S(1)}, bf16[2048,256]{1,0:T(8,128)(2,1)S(1)}, u32[]{:S(2)}, u32[]{:S(2)}) collective-permute-start(bf16[2048,256]{1,0:T(8,128)(2,1)S(1)} %standardize_rows.1.refs_4_.refs_0_), channel_id=1, source_target_pairs={{0,16},{8,24},{16,0},{24,8},{1,17},{9,25},{17,1},{25,9},{2,18},{10... | collective-permute-start | bytes 3145736 | tf_op jit(solution)/shard_map/ppermute | solution.py:20
  13.6 23.8 %collective-permute-start.3 = (bf16[2048,256]{1,0:T(8,128)(2,1)S(1)}, bf16[2048,256]{1,0:T(8,128)(2,1)S(1)}, u32[]{:S(2)}, u32[]{:S(2)}) collective-permute-start(bf16[2048,256]{1,0:T(8,128)(2,1)S(1)} %standardize_rows.1.refs_4_.refs_0_), channel_id=1, source_target_pairs={{0,8},{8,0},{16,24},{24,16},{1,9},{9,1},{17,25},{25,17},{2,10},{10... | collective-permute-start | bytes 3145736 | tf_op jit(solution)/shard_map/ppermute | solution.py:20
  15.4 16.9 %collective-permute-start.5 = (bf16[256,768]{1,0:T(8,128)(2,1)S(1)}, bf16[256,768]{1,0:T(8,128)(2,1)S(1)}, u32[]{:S(2)}, u32[]{:S(2)}) collective-permute-start(bf16[256,768]{1,0:T(8,128)(2,1)S(1)} %standardize_block.4.refs_5_.refs_0_), channel_id=1, source_target_pairs={{0,2},{1,3},{2,0},{3,1},{4,6},{5,7},{6,4},{7,5},{8,10},{9,11},{10,... | collective-permute-start | bytes 1179656 | tf_op jit(solution)/shard_map/ppermute | solution.py:20
  17.9 18.2 %collective-permute-start.12 = (bf16[512,768]{1,0:T(8,128)(2,1)S(1)}, bf16[512,768]{1,0:T(8,128)(2,1)S(1)}, u32[]{:S(2)}, u32[]{:S(2)}) collective-permute-start(bf16[512,768]{1,0:T(8,128)(2,1)S(1)} %stack_blocks.7.refs_2_), channel_id=1, source_target_pairs={{2,4},{3,5},{4,2},{5,3},{10,12},{11,13},{12,10},{13,11},{18,20},{1... | collective-permute-start | bytes 2359304 | tf_op jit(solution)/shard_map/ppermute | solution.py:20
  21.5 10.7 %collective-permute-start.7 = (bf16[256,512]{1,0:T(8,128)(2,1)S(1)}, bf16[256,512]{1,0:T(8,128)(2,1)S(1)}, u32[]{:S(2)}, u32[]{:S(2)}) collective-permute-start(bf16[256,512]{1,0:T(8,128)(2,1)S(1)} %standardize_block.5.refs_0_), channel_id=1, source_target_pairs={{0,2},{1,3},{2,0},{3,1},{4,6},{5,7},{6,4},{7,5},{8,10},{9,11},{10,... | collective-permute-start | bytes 786440 | tf_op jit(solution)/shard_map/ppermute | solution.py:20
  32.3 21.9 %collective-permute-start.14 = (bf16[512,768]{1,0:T(8,128)(2,1)S(1)}, bf16[512,768]{1,0:T(8,128)(2,1)S(1)}, u32[]{:S(2)}, u32[]{:S(2)}) collective-permute-start(bf16[512,768]{1,0:T(8,128)(2,1)S(1)} %stack_blocks.8.refs_0_.refs_2_), channel_id=1, source_target_pairs={{2,4},{3,5},{4,2},{5,3},{10,12},{11,13},{12,10},{13,11},{18,20},{1... | collective-permute-start | bytes 2359304 | tf_op jit(solution)/shard_map/ppermute | solution.py:20
  36.1 23.5 %collective-permute-start.13 = (bf16[512,768]{1,0:T(8,128)(2,1)S(1)}, bf16[512,768]{1,0:T(8,128)(2,1)S(1)}, u32[]{:S(2)}, u32[]{:S(2)}) collective-permute-start(bf16[512,768]{1,0:T(8,128)(2,1)S(1)} %collective-permute-done.12.refs_2_), channel_id=1, source_target_pairs={{2,0},{3,1},{4,6},{5,7},{10,8},{11,9},{12,14},{13,15},{18,16},{19,... | collective-permute-start | bytes 2359304 | tf_op jit(solution)/shard_map/ppermute | solution.py:20
  37.5 21.4 %collective-permute-start.8 = (bf16[1024,256]{1,0:T(8,128)(2,1)S(1)}, bf16[1024,256]{1,0:T(8,128)(2,1)S(1)}, u32[]{:S(2)}, u32[]{:S(2)}) collective-permute-start(bf16[1024,256]{1,0:T(8,128)(2,1)S(1)} %get-tuple-element.29), channel_id=1, source_target_pairs={{0,16},{8,24},{16,0},{24,8},{1,17},{9,25},{17,1},{25,9},{2,18},{10... | collective-permute-start | bytes 1572872 | tf_op jit(solution)/shard_map/ppermute | solution.py:20
  38.4 20.6 %collective-permute-start.9 = (bf16[1024,256]{1,0:T(8,128)(2,1)S(1)}, bf16[1024,256]{1,0:T(8,128)(2,1)S(1)}, u32[]{:S(2)}, u32[]{:S(2)}) collective-permute-start(bf16[1024,256]{1,0:T(8,128)(2,1)S(1)} %get-tuple-element.30), channel_id=1, source_target_pairs={{0,8},{8,0},{16,24},{24,16},{1,9},{9,1},{17,25},{25,17},{2,10},{10... | collective-permute-start | bytes 1572872 | tf_op jit(solution)/shard_map/ppermute | solution.py:20
  54.2 16.0 %collective-permute-start.18 = (bf16[512,768]{1,0:T(8,128)(2,1)S(1)}, bf16[512,768]{1,0:T(8,128)(2,1)S(1)}, u32[]{:S(2)}, u32[]{:S(2)}) collective-permute-start(bf16[512,768]{1,0:T(8,128)(2,1)S(1)} %collective-permute-done.14.refs_6_.refs_2_), channel_id=1, source_target_pairs={{2,0},{3,1},{4,6},{5,7},{10,8},{11,9},{12,14},{13,15},{18,16},{19,... | collective-permute-start | bytes 2359304 | tf_op jit(solution)/shard_map/ppermute | solution.py:20
  55.6 12.9 %collective-permute-start.10 = (bf16[512,512]{1,0:T(8,128)(2,1)S(1)}, bf16[512,512]{1,0:T(8,128)(2,1)S(1)}, u32[]{:S(2)}, u32[]{:S(2)}) collective-permute-start(bf16[512,512]{1,0:T(8,128)(2,1)S(1)} %stack_blocks.10.refs_5_.refs_6_), channel_id=1, source_target_pairs={{2,4},{3,5},{4,2},{5,3},{10,12},{11,13},{12,10},{13,11},{18,20},{1... | collective-permute-start | bytes 1572872 | tf_op jit(solution)/shard_map/ppermute | solution.py:20
  59.8 10.6 %collective-permute-start.15 = (bf16[256,768]{1,0:T(8,128)(2,1)S(1)}, bf16[256,768]{1,0:T(8,128)(2,1)S(1)}, u32[]{:S(2)}, u32[]{:S(2)}) collective-permute-start(bf16[256,768]{1,0:T(8,128)(2,1)S(1)} %get-tuple-element.32), channel_id=1, source_target_pairs={{0,8},{8,0},{16,24},{24,16},{1,9},{9,1},{17,25},{25,17},{2,10},{10... | collective-permute-start | bytes 1179656 | tf_op jit(solution)/shard_map/ppermute | solution.py:20
  60.7 9.7 %collective-permute-start.16 = (bf16[256,768]{1,0:T(8,128)(2,1)S(1)}, bf16[256,768]{1,0:T(8,128)(2,1)S(1)}, u32[]{:S(2)}, u32[]{:S(2)}) collective-permute-start(bf16[256,768]{1,0:T(8,128)(2,1)S(1)} %get-tuple-element.33), channel_id=1, source_target_pairs={{0,16},{8,24},{16,0},{24,8},{1,17},{9,25},{17,1},{25,9},{2,18},{10... | collective-permute-start | bytes 1179656 | tf_op jit(solution)/shard_map/ppermute | solution.py:20
  61.4 15.1 %collective-permute-start.17 = (bf16[256,768]{1,0:T(8,128)(2,1)S(1)}, bf16[256,768]{1,0:T(8,128)(2,1)S(1)}, u32[]{:S(2)}, u32[]{:S(2)}) collective-permute-start(bf16[256,768]{1,0:T(8,128)(2,1)S(1)} %get-tuple-element.34), channel_id=1, source_target_pairs={{0,24},{8,16},{16,8},{24,0},{1,25},{9,17},{17,9},{25,1},{2,26},{10... | collective-permute-start | bytes 1179656 | tf_op jit(solution)/shard_map/ppermute | solution.py:20
  76.7 8.2 %collective-permute-start.19 = (bf16[1024,768]{1,0:T(8,128)(2,1)S(1)}, bf16[1024,768]{1,0:T(8,128)(2,1)S(1)}, u32[]{:S(2)}, u32[]{:S(2)}) collective-permute-start(bf16[1024,768]{1,0:T(8,128)(2,1)S(1)} %stack_blocks.11.refs_0_), channel_id=1, source_target_pairs={{1,0},{0,1},{3,2},{2,3},{5,4},{4,5},{7,6},{6,7},{9,8},{8,9},{11,10... | collective-permute-start | bytes 4718600 | tf_op jit(solution)/shard_map/ppermute | solution.py:20
  80.9 14.4 %collective-permute-start.11 = (bf16[512,512]{1,0:T(8,128)(2,1)S(1)}, bf16[512,512]{1,0:T(8,128)(2,1)S(1)}, u32[]{:S(2)}, u32[]{:S(2)}) collective-permute-start(bf16[512,512]{1,0:T(8,128)(2,1)S(1)} %collective-permute-done.10.refs_7_.refs_2_), channel_id=1, source_target_pairs={{2,0},{3,1},{4,6},{5,7},{10,8},{11,9},{12,14},{13,15},{18,16},{19,... | collective-permute-start | bytes 1572872 | tf_op jit(solution)/shard_map/ppermute | solution.py:20
  82.2 13.5 %collective-permute-start.23 = (bf16[256,768]{1,0:T(8,128)(2,1)S(1)}, bf16[256,768]{1,0:T(8,128)(2,1)S(1)}, u32[]{:S(2)}, u32[]{:S(2)}) collective-permute-start(bf16[256,768]{1,0:T(8,128)(2,1)S(1)} %get-tuple-element.41), channel_id=1, source_target_pairs={{0,8},{8,0},{16,24},{24,16},{1,9},{9,1},{17,25},{25,17},{2,10},{10... | collective-permute-start | bytes 1179656 | tf_op jit(solution)/shard_map/ppermute | solution.py:20
  82.9 12.8 %collective-permute-start.24 = (bf16[256,768]{1,0:T(8,128)(2,1)S(1)}, bf16[256,768]{1,0:T(8,128)(2,1)S(1)}, u32[]{:S(2)}, u32[]{:S(2)}) collective-permute-start(bf16[256,768]{1,0:T(8,128)(2,1)S(1)} %get-tuple-element.42), channel_id=1, source_target_pairs={{0,16},{8,24},{16,0},{24,8},{1,17},{9,25},{17,1},{25,9},{2,18},{10... | collective-permute-start | bytes 1179656 | tf_op jit(solution)/shard_map/ppermute | solution.py:20
  83.7 18.2 %collective-permute-start.25 = (bf16[256,768]{1,0:T(8,128)(2,1)S(1)}, bf16[256,768]{1,0:T(8,128)(2,1)S(1)}, u32[]{:S(2)}, u32[]{:S(2)}) collective-permute-start(bf16[256,768]{1,0:T(8,128)(2,1)S(1)} %get-tuple-element.43), channel_id=1, source_target_pairs={{0,24},{8,16},{16,8},{24,0},{1,25},{9,17},{17,9},{25,1},{2,26},{10... | collective-permute-start | bytes 1179656 | tf_op jit(solution)/shard_map/ppermute | solution.py:20
  102.0 4.1 %collective-permute-start.26 = (bf16[1024,768]{1,0:T(8,128)(2,1)S(1)}, bf16[1024,768]{1,0:T(8,128)(2,1)S(1)}, u32[]{:S(2)}, u32[]{:S(2)}) collective-permute-start(bf16[1024,768]{1,0:T(8,128)(2,1)S(1)} %stack_blocks.12.refs_0_), channel_id=1, source_target_pairs={{1,0},{0,1},{3,2},{2,3},{5,4},{4,5},{7,6},{6,7},{9,8},{8,9},{11,10... | collective-permute-start | bytes 4718600 | tf_op jit(solution)/shard_map/ppermute | solution.py:20
  103.0 13.4 %collective-permute-start.20 = (bf16[256,512]{1,0:T(8,128)(2,1)S(1)}, bf16[256,512]{1,0:T(8,128)(2,1)S(1)}, u32[]{:S(2)}, u32[]{:S(2)}) collective-permute-start(bf16[256,512]{1,0:T(8,128)(2,1)S(1)} %get-tuple-element.38), channel_id=1, source_target_pairs={{0,8},{8,0},{16,24},{24,16},{1,9},{9,1},{17,25},{25,17},{2,10},{10... | collective-permute-start | bytes 786440 | tf_op jit(solution)/shard_map/ppermute | solution.py:20
  103.9 12.5 %collective-permute-start.21 = (bf16[256,512]{1,0:T(8,128)(2,1)S(1)}, bf16[256,512]{1,0:T(8,128)(2,1)S(1)}, u32[]{:S(2)}, u32[]{:S(2)}) collective-permute-start(bf16[256,512]{1,0:T(8,128)(2,1)S(1)} %get-tuple-element.39), channel_id=1, source_target_pairs={{0,16},{8,24},{16,0},{24,8},{1,17},{9,25},{17,1},{25,9},{2,18},{10... | collective-permute-start | bytes 786440 | tf_op jit(solution)/shard_map/ppermute | solution.py:20
  104.6 12.5 %collective-permute-start.22 = (bf16[256,512]{1,0:T(8,128)(2,1)S(1)}, bf16[256,512]{1,0:T(8,128)(2,1)S(1)}, u32[]{:S(2)}, u32[]{:S(2)}) collective-permute-start(bf16[256,512]{1,0:T(8,128)(2,1)S(1)} %get-tuple-element.40), channel_id=1, source_target_pairs={{0,24},{8,16},{16,8},{24,0},{1,25},{9,17},{17,9},{25,1},{2,26},{10... | collective-permute-start | bytes 786440 | tf_op jit(solution)/shard_map/ppermute | solution.py:20
  117.2 5.6 %collective-permute-start.27 = (bf16[1024,512]{1,0:T(8,128)(2,1)S(1)}, bf16[1024,512]{1,0:T(8,128)(2,1)S(1)}, u32[]{:S(2)}, u32[]{:S(2)}) collective-permute-start(bf16[1024,512]{1,0:T(8,128)(2,1)S(1)} %stack_blocks.13.refs_0_), channel_id=1, source_target_pairs={{1,0},{0,1},{3,2},{2,3},{5,4},{4,5},{7,6},{6,7},{9,8},{8,9},{11,10... | collective-permute-start | bytes 3145736 | tf_op jit(solution)/shard_map/ppermute | solution.py:20
where the time goes:
time: 127 us
  waiting for transfers between devices  52.3 us (41%)
  starting transfers between devices  37.6 us (30%)
  Pallas kernels  35.2 us (28%)
  local copies, waits for them, and re-layouts  1.6 us (1%)
    ppermute x28, waiting for transfers between devices, send(): return lax.ppermute(x, axis, pairs)  52.3 us
    ppermute x28, starting transfers between devices, send(): return lax.ppermute(x, axis, pairs)  37.6 us
    pallas_call x4, Pallas kernels, gram_part(): call(functools.partial(gram_kernel, inner, steps, start, scale), 'gram_pa...  29.3 us
    pallas_call x4, Pallas kernels, standardize(): call(functools.partial(kernel, len(terms)), name, (20 * size, 6 * size, s...  3.7 us
  transfers between devices with their start and end apart: 28, of which 12 were waited for; matrix products, arithmetic and copies ran while one was open for 0% of the time, Pallas kernels for 24%

commit v1 on v0

--- a/solution.py
+++ b/solution.py
@@ -8,7 +8,7 @@
 from jax.sharding import PartitionSpec as P
 
 STRIP = 128
-SHARES = (3, 3, 2)
+SHARES = (2, 2, 2, 2)
 TILE = 1024
 MIB = 2**20
 SLACK = 8
@@ -389,7 +389,7 @@
             )
     lines, boths = [], []
     for q, (block, near) in enumerate(zip(blocks, nears)):
-        after = boths[-1:] + (nears[q + 1 :] if q else [])
+        after = boths[-1:] + (nears[q + 1 : q + 2] if q else [])
         both, arrays = line_gather(block, near, outer, inner, after)
         lines.append(arrays)
         boths.append(both)

time: 127 us -> 129 us (1.016)
  the two profiles are of different devices: /device:TPU:9 before, /device:TPU:0 now
where the time goes in v1:
time: 129 us; the launch traced here: 128 us
  waiting for transfers between devices  49.2 us (38%)
  starting transfers between devices  41.5 us (32%)
  Pallas kernels  34.1 us (26%)
  local copies, waits for them, and re-layouts  2.98 us (2%)
    ppermute x35, waiting for transfers between devices, send(): return lax.ppermute(x, axis, pairs)  49.2 us
    ppermute x35, starting transfers between devices, send(): return lax.ppermute(x, axis, pairs)  41.5 us
    pallas_call x5, Pallas kernels, gram_part(): call(functools.partial(gram_kernel, inner, steps, start, scale), 'gram_pa...  28 us
    pallas_call x5, Pallas kernels, standardize(): call(functools.partial(kernel, len(terms)), name, (20 * size, 6 * size, s...  3.81 us
    unnamed x6, local copies, waits for them, and re-layouts  2.98 us
  transfers between devices with their start and end apart: 35, of which 14 were waited for; matrix products, arithmetic and copies ran while one was open for 0% of the time, Pallas kernels for 21%

profile of v1, /device:TPU:0, one launch (start us, length us, event | category | flops | bytes accessed | tf_op | source)
XLA Modules:
  0.0 128.3 jit_solution(5515331043009683539)
XLA Ops:
  0.0 1.6 %copy-done = f32[256,2048]{1,0:T(8,128)S(1)} copy-done((f32[256,2048]{1,0:T(8,128)S(1)}, f32[256,2048]{1,0:T(8,128)}, u32[]{:S(2)}) %copy-start) | copy-done | bytes 2097176
  3.2 2.9 %collective-permute-start.1 = (f32[8,256]{1,0:T(8,128)S(1)}, f32[8,256]{1,0:T(8,128)S(1)}, u32[]{:S(2)}, u32[]{:S(2)}) collective-permute-start(f32[8,256]{1,0:T(8,128)S(1)} %add_terms.2.a_ref), channel_id=1, source_target_pairs={{0,2},{1,3},{2,0},{3,1},{4,6},{5,7},{6,4},{7,5},{8,10},{9,11},{10,... | collective-permute-start | bytes 24584 | tf_op jit(solution)/shard_map/ppermute | solution.py:20
  6.1 1.6 %collective-permute-done.1.b_ref = f32[8,256]{1,0:T(8,128)S(1)} collective-permute-done((f32[8,256]{1,0:T(8,128)S(1)}, f32[8,256]{1,0:T(8,128)S(1)}, u32[]{:S(2)}, u32[]{:S(2)}) %collective-permute-start.1) | collective-permute-done | bytes 8224 | tf_op jit(solution)/shard_map/ppermute | solution.py:20
  7.7 3.0 %collective-permute-start.2 = (f32[8,256]{1,0:T(8,128)S(1)}, f32[8,256]{1,0:T(8,128)S(1)}, u32[]{:S(2)}, u32[]{:S(2)}) collective-permute-start(f32[8,256]{1,0:T(8,128)S(1)} %add_terms.3.refs_0_.refs_2_), channel_id=1, source_target_pairs={{0,4},{1,5},{2,6},{3,7},{4,0},{5,1},{6,2},{7,3},{8,12},{9,13},{10,... | collective-permute-start | bytes 24584 | tf_op jit(solution)/shard_map/ppermute | solution.py:20
  12.8 2.3 %standardize_rows.1.refs_4_.refs_0_ = bf16[2048,256]{1,0:T(8,128)(2,1)S(1)} custom-call(f32[256,2048]{1,0:T(8,128)S(1)} %get-tuple-element.33.refs_0_.counts_ref, f32[16,2048]{1,0:T(8,128)S(1)} %gene_scales.1.refs_1_.genes_ref, f32[8,256]{1,0:T(8,128)S(1)} %add_terms.3.refs_0_.refs_2_, f32[8,256]{1,0:T(8,128)S(1)} %collective-permute-done.2.refs_3_.refs_1_, ...), custom_call_target="tpu_custom_call" | custom-call | flops 1310720 | bytes 393216 | tf_op jit(solution)/shard_map/standardize_rows/pallas_call | solution.py:147
  15.0 1.9 %collective-permute-start.3 = (bf16[2048,256]{1,0:T(8,128)(2,1)S(1)}, bf16[2048,256]{1,0:T(8,128)(2,1)S(1)}, u32[]{:S(2)}, u32[]{:S(2)}) collective-permute-start(bf16[2048,256]{1,0:T(8,128)(2,1)S(1)} %standardize_rows.1.refs_4_.refs_0_), channel_id=1, source_target_pairs={{0,8},{8,0},{16,24},{24,16},{1,9},{9,1},{17,25},{25,17},{2,10},{10... | collective-permute-start | bytes 3145736 | tf_op jit(solution)/shard_map/ppermute | solution.py:20
  16.9 1.5 %collective-permute-start.4 = (bf16[2048,256]{1,0:T(8,128)(2,1)S(1)}, bf16[2048,256]{1,0:T(8,128)(2,1)S(1)}, u32[]{:S(2)}, u32[]{:S(2)}) collective-permute-start(bf16[2048,256]{1,0:T(8,128)(2,1)S(1)} %standardize_rows.1.refs_4_.refs_0_), channel_id=1, source_target_pairs={{0,16},{8,24},{16,0},{24,8},{1,17},{9,25},{17,1},{25,9},{2,18},{10... | collective-permute-start | bytes 3145736 | tf_op jit(solution)/shard_map/ppermute | solution.py:20
  18.4 1.6 %collective-permute-start.6 = (bf16[256,512]{1,0:T(8,128)(2,1)S(1)}, bf16[256,512]{1,0:T(8,128)(2,1)S(1)}, u32[]{:S(2)}, u32[]{:S(2)}) collective-permute-start(bf16[256,512]{1,0:T(8,128)(2,1)S(1)} %standardize_block.4.refs_2_.refs_0_), channel_id=1, source_target_pairs={{0,2},{1,3},{2,0},{3,1},{4,6},{5,7},{6,4},{7,5},{8,10},{9,11},{10,... | collective-permute-start | bytes 786440 | tf_op jit(solution)/shard_map/ppermute | solution.py:20
  21.3 1.6 %collective-permute-start.7 = (bf16[256,512]{1,0:T(8,128)(2,1)S(1)}, bf16[256,512]{1,0:T(8,128)(2,1)S(1)}, u32[]{:S(2)}, u32[]{:S(2)}) collective-permute-start(bf16[256,512]{1,0:T(8,128)(2,1)S(1)} %standardize_block.6.refs_6_.refs_0_), channel_id=1, source_target_pairs={{0,2},{1,3},{2,0},{3,1},{4,6},{5,7},{6,4},{7,5},{8,10},{9,11},{10,... | collective-permute-start | bytes 786440 | tf_op jit(solution)/shard_map/ppermute | solution.py:20
  23.0 4.7 %collective-permute-done.6.refs_1_ = bf16[256,512]{1,0:T(8,128)(2,1)S(1)} collective-permute-done((bf16[256,512]{1,0:T(8,128)(2,1)S(1)}, bf16[256,512]{1,0:T(8,128)(2,1)S(1)}, u32[]{:S(2)}, u32[]{:S(2)}) %collective-permute-start.6) | collective-permute-done | bytes 262176 | tf_op jit(solution)/shard_map/ppermute | solution.py:20
  28.4 7.1 %collective-permute-done.7.refs_3_.refs_1_ = bf16[256,512]{1,0:T(8,128)(2,1)S(1)} collective-permute-done((bf16[256,512]{1,0:T(8,128)(2,1)S(1)}, bf16[256,512]{1,0:T(8,128)(2,1)S(1)}, u32[]{:S(2)}, u32[]{:S(2)}) %collective-permute-start.7) | collective-permute-done | bytes 262176 | tf_op jit(solution)/shard_map/ppermute | solution.py:20
  36.7 4.1 %collective-permute-start.10 = (bf16[256,512]{1,0:T(8,128)(2,1)S(1)}, bf16[256,512]{1,0:T(8,128)(2,1)S(1)}, u32[]{:S(2)}, u32[]{:S(2)}) collective-permute-start(bf16[256,512]{1,0:T(8,128)(2,1)S(1)} %standardize_block.7.refs_0_), channel_id=1, source_target_pairs={{0,2},{1,3},{2,0},{3,1},{4,6},{5,7},{6,4},{7,5},{8,10},{9,11},{10,... | collective-permute-start | bytes 786440 | tf_op jit(solution)/shard_map/ppermute | solution.py:20
  43.6 3.7 %collective-permute-done.10.refs_3_.refs_1_ = bf16[256,512]{1,0:T(8,128)(2,1)S(1)} collective-permute-done((bf16[256,512]{1,0:T(8,128)(2,1)S(1)}, bf16[256,512]{1,0:T(8,128)(2,1)S(1)}, u32[]{:S(2)}, u32[]{:S(2)}) %collective-permute-start.10) | collective-permute-done | bytes 262176 | tf_op jit(solution)/shard_map/ppermute | solution.py:20
  48.0 1.3 %collective-permute-start.14 = (bf16[512,512]{1,0:T(8,128)(2,1)S(1)}, bf16[512,512]{1,0:T(8,128)(2,1)S(1)}, u32[]{:S(2)}, u32[]{:S(2)}) collective-permute-start(bf16[512,512]{1,0:T(8,128)(2,1)S(1)} %collective-permute-done.13.refs_6_.refs_2_), channel_id=1, source_target_pairs={{2,0},{3,1},{4,6},{5,7},{10,8},{11,9},{12,14},{13,15},{18,16},{19,... | collective-permute-start | bytes 1572872 | tf_op jit(solution)/shard_map/ppermute | solution.py:20
  49.4 1.8 %collective-permute-done.8.refs_3_ = bf16[1024,256]{1,0:T(8,128)(2,1)S(1)} collective-permute-done((bf16[1024,256]{1,0:T(8,128)(2,1)S(1)}, bf16[1024,256]{1,0:T(8,128)(2,1)S(1)}, u32[]{:S(2)}, u32[]{:S(2)}) %collective-permute-start.8) | collective-permute-done | bytes 524320 | tf_op jit(solution)/shard_map/ppermute | solution.py:20
  52.7 6.3 %collective-permute-done.16.refs_3_ = bf16[512,512]{1,0:T(8,128)(2,1)S(1)} collective-permute-done((bf16[512,512]{1,0:T(8,128)(2,1)S(1)}, bf16[512,512]{1,0:T(8,128)(2,1)S(1)}, u32[]{:S(2)}, u32[]{:S(2)}) %collective-permute-start.16) | collective-permute-done | bytes 524320 | tf_op jit(solution)/shard_map/ppermute | solution.py:20
  59.2 1.6 %collective-permute-start.21 = (bf16[256,512]{1,0:T(8,128)(2,1)S(1)}, bf16[256,512]{1,0:T(8,128)(2,1)S(1)}, u32[]{:S(2)}, u32[]{:S(2)}) collective-permute-start(bf16[256,512]{1,0:T(8,128)(2,1)S(1)} %get-tuple-element.42), channel_id=1, source_target_pairs={{0,8},{8,0},{16,24},{24,16},{1,9},{9,1},{17,25},{25,17},{2,10},{10... | collective-permute-start | bytes 786440 | tf_op jit(solution)/shard_map/ppermute | solution.py:20
  62.8 4.8 %collective-permute-done.14.refs_3_ = bf16[512,512]{1,0:T(8,128)(2,1)S(1)} collective-permute-done((bf16[512,512]{1,0:T(8,128)(2,1)S(1)}, bf16[512,512]{1,0:T(8,128)(2,1)S(1)}, u32[]{:S(2)}, u32[]{:S(2)}) %collective-permute-start.14) | collective-permute-done | bytes 524320 | tf_op jit(solution)/shard_map/ppermute | solution.py:20
  67.8 2.2 %collective-permute-done.22.refs_2_ = bf16[256,512]{1,0:T(8,128)(2,1)S(1)} collective-permute-done((bf16[256,512]{1,0:T(8,128)(2,1)S(1)}, bf16[256,512]{1,0:T(8,128)(2,1)S(1)}, u32[]{:S(2)}, u32[]{:S(2)}) %collective-permute-start.22) | collective-permute-done | bytes 262176 | tf_op jit(solution)/shard_map/ppermute | solution.py:20
  70.8 1.3 %collective-permute-start.25 = (bf16[512,512]{1,0:T(8,128)(2,1)S(1)}, bf16[512,512]{1,0:T(8,128)(2,1)S(1)}, u32[]{:S(2)}, u32[]{:S(2)}) collective-permute-start(bf16[512,512]{1,0:T(8,128)(2,1)S(1)} %collective-permute-done.17.refs_7_.refs_2_), channel_id=1, source_target_pairs={{2,0},{3,1},{4,6},{5,7},{10,8},{11,9},{12,14},{13,15},{18,16},{19,... | collective-permute-start | bytes 1572872 | tf_op jit(solution)/shard_map/ppermute | solution.py:20
  73.9 1.8 %collective-permute-start.20 = (bf16[256,512]{1,0:T(8,128)(2,1)S(1)}, bf16[256,512]{1,0:T(8,128)(2,1)S(1)}, u32[]{:S(2)}, u32[]{:S(2)}) collective-permute-start(bf16[256,512]{1,0:T(8,128)(2,1)S(1)} %get-tuple-element.41), channel_id=1, source_target_pairs={{0,24},{8,16},{16,8},{24,0},{1,25},{9,17},{17,9},{25,1},{2,26},{10... | collective-permute-start | bytes 786440 | tf_op jit(solution)/shard_map/ppermute | solution.py:20
  75.7 6.4 %gram_part.5 = (f32[2048,4096]{1,0:T(8,128)}, f32[8,128]{1,0:T(8,128)S(1)}) custom-call(bf16[2048,1024]{1,0:T(8,128)(2,1)S(1)} %stack_blocks.11.refs_4_.rows_ref, bf16[1024,512]{1,0:T(8,128)(2,1)S(1)} %stack_blocks.14.refs_0_, bf16[1024,512]{1,0:T(8,128)(2,1)S(1)} %collective-permute-done.24.refs_1_, ...), custom_call_target="tpu_custom_call" | custom-call | flops 536870912 | bytes 1572864 | tf_op jit(solution)/shard_map/gram_part/pallas_call | solution.py:333
  82.1 4.9 %collective-permute-done.25.refs_3_ = bf16[512,512]{1,0:T(8,128)(2,1)S(1)} collective-permute-done((bf16[512,512]{1,0:T(8,128)(2,1)S(1)}, bf16[512,512]{1,0:T(8,128)(2,1)S(1)}, u32[]{:S(2)}, u32[]{:S(2)}) %collective-permute-start.25) | collective-permute-done | bytes 524320 | tf_op jit(solution)/shard_map/ppermute | solution.py:20
  87.4 1.3 %collective-permute-start.12 = (bf16[512,512]{1,0:T(8,128)(2,1)S(1)}, bf16[512,512]{1,0:T(8,128)(2,1)S(1)}, u32[]{:S(2)}, u32[]{:S(2)}) collective-permute-start(bf16[512,512]{1,0:T(8,128)(2,1)S(1)} %collective-permute-done.11.refs_7_.refs_2_), channel_id=1, source_target_pairs={{2,0},{3,1},{4,6},{5,7},{10,8},{11,9},{12,14},{13,15},{18,16},{19,... | collective-permute-start | bytes 1572872 | tf_op jit(solution)/shard_map/ppermute | solution.py:20
  90.9 1.4 %collective-permute-start.32 = (bf16[256,512]{1,0:T(8,128)(2,1)S(1)}, bf16[256,512]{1,0:T(8,128)(2,1)S(1)}, u32[]{:S(2)}, u32[]{:S(2)}) collective-permute-start(bf16[256,512]{1,0:T(8,128)(2,1)S(1)} %get-tuple-element.55), channel_id=1, source_target_pairs={{0,24},{8,16},{16,8},{24,0},{1,25},{9,17},{17,9},{25,1},{2,26},{10... | collective-permute-start | bytes 786440 | tf_op jit(solution)/shard_map/ppermute | solution.py:20
  92.3 6.4 %gram_part.6 = (f32[2048,4096]{1,0:T(8,128)}, f32[8,128]{1,0:T(8,128)S(1)}) custom-call(bf16[2048,1024]{1,0:T(8,128)(2,1)S(1)} %stack_blocks.11.refs_4_.rows_ref, bf16[1024,512]{1,0:T(8,128)(2,1)S(1)} %stack_blocks.15.refs_0_, bf16[1024,512]{1,0:T(8,128)(2,1)S(1)} %collective-permute-done.26.refs_1_, ...), custom_call_target="tpu_custom_call", output_to_operand_aliasing={{0}: (4, {})} | custom-call | flops 536870912 | bytes 1572864 | tf_op jit(solution)/shard_map/gram_part/pallas_call | solution.py:333
  98.7 4.9 %collective-permute-done.12.refs_3_ = bf16[512,512]{1,0:T(8,128)(2,1)S(1)} collective-permute-done((bf16[512,512]{1,0:T(8,128)(2,1)S(1)}, bf16[512,512]{1,0:T(8,128)(2,1)S(1)}, u32[]{:S(2)}, u32[]{:S(2)}) %collective-permute-start.12) | collective-permute-done | bytes 524320 | tf_op jit(solution)/shard_map/ppermute | solution.py:20
  106.4 1.3 %collective-permute-start.29 = (bf16[256,512]{1,0:T(8,128)(2,1)S(1)}, bf16[256,512]{1,0:T(8,128)(2,1)S(1)}, u32[]{:S(2)}, u32[]{:S(2)}) collective-permute-start(bf16[256,512]{1,0:T(8,128)(2,1)S(1)} %get-tuple-element.52), channel_id=1, source_target_pairs={{0,24},{8,16},{16,8},{24,0},{1,25},{9,17},{17,9},{25,1},{2,26},{10... | collective-permute-start | bytes 786440 | tf_op jit(solution)/shard_map/ppermute | solution.py:20
  107.8 6.4 %gram_part.7 = (f32[2048,4096]{1,0:T(8,128)}, f32[8,128]{1,0:T(8,128)S(1)}) custom-call(bf16[2048,1024]{1,0:T(8,128)(2,1)S(1)} %stack_blocks.11.refs_4_.rows_ref, bf16[1024,512]{1,0:T(8,128)(2,1)S(1)} %stack_blocks.16.refs_0_, bf16[1024,512]{1,0:T(8,128)(2,1)S(1)} %collective-permute-done.33.refs_1_, ...), custom_call_target="tpu_custom_call", output_to_operand_aliasing={{0}: (4, {})} | custom-call | flops 536870912 | bytes 1572864 | tf_op jit(solution)/shard_map/gram_part/pallas_call | solution.py:333
  114.2 5.1 %collective-permute-done.28.refs_2_ = bf16[256,512]{1,0:T(8,128)(2,1)S(1)} collective-permute-done((bf16[256,512]{1,0:T(8,128)(2,1)S(1)}, bf16[256,512]{1,0:T(8,128)(2,1)S(1)}, u32[]{:S(2)}, u32[]{:S(2)}) %collective-permute-start.28) | collective-permute-done | bytes 262176 | tf_op jit(solution)/shard_map/ppermute | solution.py:20
  119.4 4.4 %gram_part.8 = (f32[2048,4096]{1,0:T(8,128)}, f32[8,128]{1,0:T(8,128)}) custom-call(bf16[2048,1024]{1,0:T(8,128)(2,1)S(1)} %stack_blocks.11.refs_4_.rows_ref, bf16[1024,512]{1,0:T(8,128)(2,1)S(1)} %stack_blocks.17.refs_0_, f32[2048,4096]{1,0:T(8,128)} %get-tuple-element.58.refs_1_), custom_call_target="tpu_custom_call", output_to_operand_aliasing={{0}: (2, {})} | custom-call | flops 268435456 | bytes 1048576 | tf_op jit(solution)/shard_map/gram_part/pallas_call | solution.py:333
  123.9 4.3 %gram_part.9 = (f32[2048,4096]{1,0:T(8,128)}, f32[8,128]{1,0:T(8,128)}) custom-call(bf16[2048,1024]{1,0:T(8,128)(2,1)S(1)} %stack_blocks.11.refs_4_.rows_ref, bf16[1024,512]{1,0:T(8,128)(2,1)S(1)} %collective-permute-done.34.refs_0_, f32[2048,4096]{1,0:T(8,128)} %get-tuple-element.59.refs_1_), custom_call_target="tpu_custom_call", output_to_operand_aliasing={{0}: (2, {})} | custom-call | flops 268435456 | bytes 1048576 | tf_op jit(solution)/shard_map/gram_part/pallas_call | solution.py:333
  (72 shorter events, 22.1 us)
Async XLA Ops:
  3.2 4.5 %collective-permute-start.1 = (f32[8,256]{1,0:T(8,128)S(1)}, f32[8,256]{1,0:T(8,128)S(1)}, u32[]{:S(2)}, u32[]{:S(2)}) collective-permute-start(f32[8,256]{1,0:T(8,128)S(1)} %add_terms.2.a_ref), channel_id=1, source_target_pairs={{0,2},{1,3},{2,0},{3,1},{4,6},{5,7},{6,4},{7,5},{8,10},{9,11},{10,... | collective-permute-start | bytes 24584 | tf_op jit(solution)/shard_map/ppermute | solution.py:20
  7.7 4.7 %collective-permute-start.2 = (f32[8,256]{1,0:T(8,128)S(1)}, f32[8,256]{1,0:T(8,128)S(1)}, u32[]{:S(2)}, u32[]{:S(2)}) collective-permute-start(f32[8,256]{1,0:T(8,128)S(1)} %add_terms.3.refs_0_.refs_2_), channel_id=1, source_target_pairs={{0,4},{1,5},{2,6},{3,7},{4,0},{5,1},{6,2},{7,3},{8,12},{9,13},{10,... | collective-permute-start | bytes 24584 | tf_op jit(solution)/shard_map/ppermute | solution.py:20
  15.0 25.7 %collective-permute-start.3 = (bf16[2048,256]{1,0:T(8,128)(2,1)S(1)}, bf16[2048,256]{1,0:T(8,128)(2,1)S(1)}, u32[]{:S(2)}, u32[]{:S(2)}) collective-permute-start(bf16[2048,256]{1,0:T(8,128)(2,1)S(1)} %standardize_rows.1.refs_4_.refs_0_), channel_id=1, source_target_pairs={{0,8},{8,0},{16,24},{24,16},{1,9},{9,1},{17,25},{25,17},{2,10},{10... | collective-permute-start | bytes 3145736 | tf_op jit(solution)/shard_map/ppermute | solution.py:20
  16.9 23.9 %collective-permute-start.4 = (bf16[2048,256]{1,0:T(8,128)(2,1)S(1)}, bf16[2048,256]{1,0:T(8,128)(2,1)S(1)}, u32[]{:S(2)}, u32[]{:S(2)}) collective-permute-start(bf16[2048,256]{1,0:T(8,128)(2,1)S(1)} %standardize_rows.1.refs_4_.refs_0_), channel_id=1, source_target_pairs={{0,16},{8,24},{16,0},{24,8},{1,17},{9,25},{17,1},{25,9},{2,18},{10... | collective-permute-start | bytes 3145736 | tf_op jit(solution)/shard_map/ppermute | solution.py:20
  18.4 9.2 %collective-permute-start.6 = (bf16[256,512]{1,0:T(8,128)(2,1)S(1)}, bf16[256,512]{1,0:T(8,128)(2,1)S(1)}, u32[]{:S(2)}, u32[]{:S(2)}) collective-permute-start(bf16[256,512]{1,0:T(8,128)(2,1)S(1)} %standardize_block.4.refs_2_.refs_0_), channel_id=1, source_target_pairs={{0,2},{1,3},{2,0},{3,1},{4,6},{5,7},{6,4},{7,5},{8,10},{9,11},{10,... | collective-permute-start | bytes 786440 | tf_op jit(solution)/shard_map/ppermute | solution.py:20
  20.4 15.1 %collective-permute-start.5 = (bf16[256,512]{1,0:T(8,128)(2,1)S(1)}, bf16[256,512]{1,0:T(8,128)(2,1)S(1)}, u32[]{:S(2)}, u32[]{:S(2)}) collective-permute-start(bf16[256,512]{1,0:T(8,128)(2,1)S(1)} %standardize_block.5.refs_5_.refs_0_), channel_id=1, source_target_pairs={{0,2},{1,3},{2,0},{3,1},{4,6},{5,7},{6,4},{7,5},{8,10},{9,11},{10,... | collective-permute-start | bytes 786440 | tf_op jit(solution)/shard_map/ppermute | solution.py:20
  21.3 14.2 %collective-permute-start.7 = (bf16[256,512]{1,0:T(8,128)(2,1)S(1)}, bf16[256,512]{1,0:T(8,128)(2,1)S(1)}, u32[]{:S(2)}, u32[]{:S(2)}) collective-permute-start(bf16[256,512]{1,0:T(8,128)(2,1)S(1)} %standardize_block.6.refs_6_.refs_0_), channel_id=1, source_target_pairs={{0,2},{1,3},{2,0},{3,1},{4,6},{5,7},{6,4},{7,5},{8,10},{9,11},{10,... | collective-permute-start | bytes 786440 | tf_op jit(solution)/shard_map/ppermute | solution.py:20
  27.7 14.5 %collective-permute-start.15 = (bf16[512,512]{1,0:T(8,128)(2,1)S(1)}, bf16[512,512]{1,0:T(8,128)(2,1)S(1)}, u32[]{:S(2)}, u32[]{:S(2)}) collective-permute-start(bf16[512,512]{1,0:T(8,128)(2,1)S(1)} %stack_blocks.9.refs_2_), channel_id=1, source_target_pairs={{2,4},{3,5},{4,2},{5,3},{10,12},{11,13},{12,10},{13,11},{18,20},{1... | collective-permute-start | bytes 1572872 | tf_op jit(solution)/shard_map/ppermute | solution.py:20
  35.6 12.5 %collective-permute-start.13 = (bf16[512,512]{1,0:T(8,128)(2,1)S(1)}, bf16[512,512]{1,0:T(8,128)(2,1)S(1)}, u32[]{:S(2)}, u32[]{:S(2)}) collective-permute-start(bf16[512,512]{1,0:T(8,128)(2,1)S(1)} %stack_blocks.10.refs_0_.refs_2_), channel_id=1, source_target_pairs={{2,4},{3,5},{4,2},{5,3},{10,12},{11,13},{12,10},{13,11},{18,20},{1... | collective-permute-start | bytes 1572872 | tf_op jit(solution)/shard_map/ppermute | solution.py:20
  36.7 10.6 %collective-permute-start.10 = (bf16[256,512]{1,0:T(8,128)(2,1)S(1)}, bf16[256,512]{1,0:T(8,128)(2,1)S(1)}, u32[]{:S(2)}, u32[]{:S(2)}) collective-permute-start(bf16[256,512]{1,0:T(8,128)(2,1)S(1)} %standardize_block.7.refs_0_), channel_id=1, source_target_pairs={{0,2},{1,3},{2,0},{3,1},{4,6},{5,7},{6,4},{7,5},{8,10},{9,11},{10,... | collective-permute-start | bytes 786440 | tf_op jit(solution)/shard_map/ppermute | solution.py:20
  40.8 10.3 %collective-permute-start.8 = (bf16[1024,256]{1,0:T(8,128)(2,1)S(1)}, bf16[1024,256]{1,0:T(8,128)(2,1)S(1)}, u32[]{:S(2)}, u32[]{:S(2)}) collective-permute-start(bf16[1024,256]{1,0:T(8,128)(2,1)S(1)} %get-tuple-element.35), channel_id=1, source_target_pairs={{0,16},{8,24},{16,0},{24,8},{1,17},{9,25},{17,1},{25,9},{2,18},{10... | collective-permute-start | bytes 1572872 | tf_op jit(solution)/shard_map/ppermute | solution.py:20
  41.8 10.3 %collective-permute-start.9 = (bf16[1024,256]{1,0:T(8,128)(2,1)S(1)}, bf16[1024,256]{1,0:T(8,128)(2,1)S(1)}, u32[]{:S(2)}, u32[]{:S(2)}) collective-permute-start(bf16[1024,256]{1,0:T(8,128)(2,1)S(1)} %get-tuple-element.36), channel_id=1, source_target_pairs={{0,8},{8,0},{16,24},{24,16},{1,9},{9,1},{17,25},{25,17},{2,10},{10... | collective-permute-start | bytes 1572872 | tf_op jit(solution)/shard_map/ppermute | solution.py:20
  42.3 16.7 %collective-permute-start.16 = (bf16[512,512]{1,0:T(8,128)(2,1)S(1)}, bf16[512,512]{1,0:T(8,128)(2,1)S(1)}, u32[]{:S(2)}, u32[]{:S(2)}) collective-permute-start(bf16[512,512]{1,0:T(8,128)(2,1)S(1)} %collective-permute-done.15.refs_2_), channel_id=1, source_target_pairs={{2,0},{3,1},{4,6},{5,7},{10,8},{11,9},{12,14},{13,15},{18,16},{19,... | collective-permute-start | bytes 1572872 | tf_op jit(solution)/shard_map/ppermute | solution.py:20
  47.3 15.5 %collective-permute-start.17 = (bf16[512,512]{1,0:T(8,128)(2,1)S(1)}, bf16[512,512]{1,0:T(8,128)(2,1)S(1)}, u32[]{:S(2)}, u32[]{:S(2)}) collective-permute-start(bf16[512,512]{1,0:T(8,128)(2,1)S(1)} %stack_blocks.12.refs_2_), channel_id=1, source_target_pairs={{2,4},{3,5},{4,2},{5,3},{10,12},{11,13},{12,10},{13,11},{18,20},{1... | collective-permute-start | bytes 1572872 | tf_op jit(solution)/shard_map/ppermute | solution.py:20
  48.0 19.6 %collective-permute-start.14 = (bf16[512,512]{1,0:T(8,128)(2,1)S(1)}, bf16[512,512]{1,0:T(8,128)(2,1)S(1)}, u32[]{:S(2)}, u32[]{:S(2)}) collective-permute-start(bf16[512,512]{1,0:T(8,128)(2,1)S(1)} %collective-permute-done.13.refs_6_.refs_2_), channel_id=1, source_target_pairs={{2,0},{3,1},{4,6},{5,7},{10,8},{11,9},{12,14},{13,15},{18,16},{19,... | collective-permute-start | bytes 1572872 | tf_op jit(solution)/shard_map/ppermute | solution.py:20
  59.2 8.6 %collective-permute-start.21 = (bf16[256,512]{1,0:T(8,128)(2,1)S(1)}, bf16[256,512]{1,0:T(8,128)(2,1)S(1)}, u32[]{:S(2)}, u32[]{:S(2)}) collective-permute-start(bf16[256,512]{1,0:T(8,128)(2,1)S(1)} %get-tuple-element.42), channel_id=1, source_target_pairs={{0,8},{8,0},{16,24},{24,16},{1,9},{9,1},{17,25},{25,17},{2,10},{10... | collective-permute-start | bytes 786440 | tf_op jit(solution)/shard_map/ppermute | solution.py:20
  60.8 9.2 %collective-permute-start.22 = (bf16[256,512]{1,0:T(8,128)(2,1)S(1)}, bf16[256,512]{1,0:T(8,128)(2,1)S(1)}, u32[]{:S(2)}, u32[]{:S(2)}) collective-permute-start(bf16[256,512]{1,0:T(8,128)(2,1)S(1)} %get-tuple-element.43), channel_id=1, source_target_pairs={{0,16},{8,24},{16,0},{24,8},{1,17},{9,25},{17,1},{25,9},{2,18},{10... | collective-permute-start | bytes 786440 | tf_op jit(solution)/shard_map/ppermute | solution.py:20
  61.9 8.0 %collective-permute-start.23 = (bf16[256,512]{1,0:T(8,128)(2,1)S(1)}, bf16[256,512]{1,0:T(8,128)(2,1)S(1)}, u32[]{:S(2)}, u32[]{:S(2)}) collective-permute-start(bf16[256,512]{1,0:T(8,128)(2,1)S(1)} %get-tuple-element.44), channel_id=1, source_target_pairs={{0,24},{8,16},{16,8},{24,0},{1,25},{9,17},{17,9},{25,1},{2,26},{10... | collective-permute-start | bytes 786440 | tf_op jit(solution)/shard_map/ppermute | solution.py:20
  70.1 12.0 %collective-permute-start.11 = (bf16[512,512]{1,0:T(8,128)(2,1)S(1)}, bf16[512,512]{1,0:T(8,128)(2,1)S(1)}, u32[]{:S(2)}, u32[]{:S(2)}) collective-permute-start(bf16[512,512]{1,0:T(8,128)(2,1)S(1)} %stack_blocks.13.refs_5_.refs_6_), channel_id=1, source_target_pairs={{2,4},{3,5},{4,2},{5,3},{10,12},{11,13},{12,10},{13,11},{18,20},{1... | collective-permute-start | bytes 1572872 | tf_op jit(solution)/shard_map/ppermute | solution.py:20
  70.8 16.2 %collective-permute-start.25 = (bf16[512,512]{1,0:T(8,128)(2,1)S(1)}, bf16[512,512]{1,0:T(8,128)(2,1)S(1)}, u32[]{:S(2)}, u32[]{:S(2)}) collective-permute-start(bf16[512,512]{1,0:T(8,128)(2,1)S(1)} %collective-permute-done.17.refs_7_.refs_2_), channel_id=1, source_target_pairs={{2,0},{3,1},{4,6},{5,7},{10,8},{11,9},{12,14},{13,15},{18,16},{19,... | collective-permute-start | bytes 1572872 | tf_op jit(solution)/shard_map/ppermute | solution.py:20
  72.1 15.1 %collective-permute-start.18 = (bf16[256,512]{1,0:T(8,128)(2,1)S(1)}, bf16[256,512]{1,0:T(8,128)(2,1)S(1)}, u32[]{:S(2)}, u32[]{:S(2)}) collective-permute-start(bf16[256,512]{1,0:T(8,128)(2,1)S(1)} %get-tuple-element.39), channel_id=1, source_target_pairs={{0,8},{8,0},{16,24},{24,16},{1,9},{9,1},{17,25},{25,17},{2,10},{10... | collective-permute-start | bytes 786440 | tf_op jit(solution)/shard_map/ppermute | solution.py:20
  72.8 14.5 %collective-permute-start.19 = (bf16[256,512]{1,0:T(8,128)(2,1)S(1)}, bf16[256,512]{1,0:T(8,128)(2,1)S(1)}, u32[]{:S(2)}, u32[]{:S(2)}) collective-permute-start(bf16[256,512]{1,0:T(8,128)(2,1)S(1)} %get-tuple-element.40), channel_id=1, source_target_pairs={{0,16},{8,24},{16,0},{24,8},{1,17},{9,25},{17,1},{25,9},{2,18},{10... | collective-permute-start | bytes 786440 | tf_op jit(solution)/shard_map/ppermute | solution.py:20
  73.9 13.4 %collective-permute-start.20 = (bf16[256,512]{1,0:T(8,128)(2,1)S(1)}, bf16[256,512]{1,0:T(8,128)(2,1)S(1)}, u32[]{:S(2)}, u32[]{:S(2)}) collective-permute-start(bf16[256,512]{1,0:T(8,128)(2,1)S(1)} %get-tuple-element.41), channel_id=1, source_target_pairs={{0,24},{8,16},{16,8},{24,0},{1,25},{9,17},{17,9},{25,1},{2,26},{10... | collective-permute-start | bytes 786440 | tf_op jit(solution)/shard_map/ppermute | solution.py:20
  87.4 4.9 %collective-permute-start.26 = (bf16[1024,512]{1,0:T(8,128)(2,1)S(1)}, bf16[1024,512]{1,0:T(8,128)(2,1)S(1)}, u32[]{:S(2)}, u32[]{:S(2)}) collective-permute-start(bf16[1024,512]{1,0:T(8,128)(2,1)S(1)} %stack_blocks.15.refs_0_), channel_id=1, source_target_pairs={{1,0},{0,1},{3,2},{2,3},{5,4},{4,5},{7,6},{6,7},{9,8},{8,9},{11,10... | collective-permute-start | bytes 3145736 | tf_op jit(solution)/shard_map/ppermute | solution.py:20
  87.4 16.2 %collective-permute-start.12 = (bf16[512,512]{1,0:T(8,128)(2,1)S(1)}, bf16[512,512]{1,0:T(8,128)(2,1)S(1)}, u32[]{:S(2)}, u32[]{:S(2)}) collective-permute-start(bf16[512,512]{1,0:T(8,128)(2,1)S(1)} %collective-permute-done.11.refs_7_.refs_2_), channel_id=1, source_target_pairs={{2,0},{3,1},{4,6},{5,7},{10,8},{11,9},{12,14},{13,15},{18,16},{19,... | collective-permute-start | bytes 1572872 | tf_op jit(solution)/shard_map/ppermute | solution.py:20
  88.7 15.3 %collective-permute-start.30 = (bf16[256,512]{1,0:T(8,128)(2,1)S(1)}, bf16[256,512]{1,0:T(8,128)(2,1)S(1)}, u32[]{:S(2)}, u32[]{:S(2)}) collective-permute-start(bf16[256,512]{1,0:T(8,128)(2,1)S(1)} %get-tuple-element.53), channel_id=1, source_target_pairs={{0,8},{8,0},{16,24},{24,16},{1,9},{9,1},{17,25},{25,17},{2,10},{10... | collective-permute-start | bytes 786440 | tf_op jit(solution)/shard_map/ppermute | solution.py:20
  89.8 14.2 %collective-permute-start.31 = (bf16[256,512]{1,0:T(8,128)(2,1)S(1)}, bf16[256,512]{1,0:T(8,128)(2,1)S(1)}, u32[]{:S(2)}, u32[]{:S(2)}) collective-permute-start(bf16[256,512]{1,0:T(8,128)(2,1)S(1)} %get-tuple-element.54), channel_id=1, source_target_pairs={{0,16},{8,24},{16,0},{24,8},{1,17},{9,25},{17,1},{25,9},{2,18},{10... | collective-permute-start | bytes 786440 | tf_op jit(solution)/shard_map/ppermute | solution.py:20
  90.9 13.1 %collective-permute-start.32 = (bf16[256,512]{1,0:T(8,128)(2,1)S(1)}, bf16[256,512]{1,0:T(8,128)(2,1)S(1)}, u32[]{:S(2)}, u32[]{:S(2)}) collective-permute-start(bf16[256,512]{1,0:T(8,128)(2,1)S(1)} %get-tuple-element.55), channel_id=1, source_target_pairs={{0,24},{8,16},{16,8},{24,0},{1,25},{9,17},{17,9},{25,1},{2,26},{10... | collective-permute-start | bytes 786440 | tf_op jit(solution)/shard_map/ppermute | solution.py:20
  104.2 10.0 %collective-permute-start.27 = (bf16[256,512]{1,0:T(8,128)(2,1)S(1)}, bf16[256,512]{1,0:T(8,128)(2,1)S(1)}, u32[]{:S(2)}, u32[]{:S(2)}) collective-permute-start(bf16[256,512]{1,0:T(8,128)(2,1)S(1)} %get-tuple-element.50), channel_id=1, source_target_pairs={{0,8},{8,0},{16,24},{24,16},{1,9},{9,1},{17,25},{25,17},{2,10},{10... | collective-permute-start | bytes 786440 | tf_op jit(solution)/shard_map/ppermute | solution.py:20
  105.3 14.0 %collective-permute-start.28 = (bf16[256,512]{1,0:T(8,128)(2,1)S(1)}, bf16[256,512]{1,0:T(8,128)(2,1)S(1)}, u32[]{:S(2)}, u32[]{:S(2)}) collective-permute-start(bf16[256,512]{1,0:T(8,128)(2,1)S(1)} %get-tuple-element.51), channel_id=1, source_target_pairs={{0,16},{8,24},{16,0},{24,8},{1,17},{9,25},{17,1},{25,9},{2,18},{10... | collective-permute-start | bytes 786440 | tf_op jit(solution)/shard_map/ppermute | solution.py:20
  106.4 12.9 %collective-permute-start.29 = (bf16[256,512]{1,0:T(8,128)(2,1)S(1)}, bf16[256,512]{1,0:T(8,128)(2,1)S(1)}, u32[]{:S(2)}, u32[]{:S(2)}) collective-permute-start(bf16[256,512]{1,0:T(8,128)(2,1)S(1)} %get-tuple-element.52), channel_id=1, source_target_pairs={{0,24},{8,16},{16,8},{24,0},{1,25},{9,17},{17,9},{25,1},{2,26},{10... | collective-permute-start | bytes 786440 | tf_op jit(solution)/shard_map/ppermute | solution.py:20
  119.4 4.5 %collective-permute-start.34 = (bf16[1024,512]{1,0:T(8,128)(2,1)S(1)}, bf16[1024,512]{1,0:T(8,128)(2,1)S(1)}, u32[]{:S(2)}, u32[]{:S(2)}) collective-permute-start(bf16[1024,512]{1,0:T(8,128)(2,1)S(1)} %stack_blocks.17.refs_0_), channel_id=1, source_target_pairs={{1,0},{0,1},{3,2},{2,3},{5,4},{4,5},{7,6},{6,7},{9,8},{8,9},{11,10... | collective-permute-start | bytes 3145736 | tf_op jit(solution)/shard_map/ppermute | solution.py:20
  (6 other events, 11.8 us)
